TPU v7x, 32 devices: a whole 2x2x4 slice. The times are simulated.
32 devices in a mesh: cfg: 2 (over x), seq: 4 (over z), wblk: 4 (over y, core).
Axes of the slice: x: 2, y: 2, z: 4, core: 2. Of those that a mesh axis runs over, the one named last changes fastest.
Arguments:
- text_tokens: bfloat16 [2, 2, 512, 3072], P('cfg', None, 'seq', 'wblk'), may hold values from -16 to 16
- image_tokens: bfloat16 [2, 4096, 3072], P(None, 'seq', 'wblk'), may hold values from -16 to 16
- pooled_vector: float32 [2, 3072], P('cfg', 'seq'), may hold values from -6 to 6
- mod_weight: bfloat16 [3072, 3, 3072], P('seq', None, 'wblk'), may hold values from -0.109375 to 0.109375
- qkv_weight: bfloat16 [3072, 3, 16, 128], P('seq', None, 'wblk'), may hold values from -0.109375 to 0.109375
- up_weight: bfloat16 [3072, 6144], P('seq', 'wblk'), may hold values from -0.109375 to 0.109375
- query_gain: float32 [128], replicated, may hold values from 0.6 to 10
- key_gain: float32 [128], replicated, may hold values from 0.6 to 10
- attn_weight: bfloat16 [2048, 3072], P('wblk', 'seq'), may hold values from -0.125 to 0.125
- down_weight: bfloat16 [6144, 3072], P('wblk', 'seq'), may hold values from -0.078125 to 0.078125
- lengths: int32 [2], replicated, may hold values from 1 to 512, as said below
- timestep: int32 [1], replicated, may hold values from 0 to 27
Outputs:
- text_out: bfloat16 [2, 2, 512, 3072], P('cfg', None, 'seq', 'wblk')
- velocity: float32 [2, 4096, 3072], P('cfg', 'seq', 'wblk')
- new_image: float32 [2, 4096, 3072], P('cfg', 'seq', 'wblk')
Inputs may be any that keep to these rules, and one draw needn't show every extreme that they name: `lengths`: some prompt has all 512 text tokens live in every draw.
All inputs are finite; a program needn't handle non-finite values.
Results may differ from a plain program's by a relative error of at most 0.025.
Values may be sent and summed in bfloat16 or wider, within the bound.
A program may use at most 320 MiB of HBM per device.

v0:
```python
import math

import jax
import jax.numpy as jnp
from jax import lax
from jax.sharding import PartitionSpec as P

D = 3072
HD = 128
GRID = 64
STEPS = 28


epsilon = 1e-06
guidance = 3.5
time_shift = 3.0
rope_theta = 10000.0


def plan(timestep):
    step_index = timestep[0].astype(jnp.float32)
    time_now = 1.0 - step_index / STEPS
    time_next = 1.0 - (step_index + 1.0) / STEPS
    sigma_now = time_shift * time_now / (1.0 + (time_shift - 1.0) * time_now)
    sigma_next = time_shift * time_next / (1.0 + (time_shift - 1.0) * time_next)
    return (sigma_now, sigma_next - sigma_now)


def time_embedding(sigma_now, dim_count):
    halfwidth = dim_count // 2
    frequency = jnp.exp(-math.log(10000.0) * jnp.arange(halfwidth, dtype=jnp.float32) / halfwidth)
    angles = 1000.0 * sigma_now * frequency
    return jnp.concatenate([jnp.cos(angles), jnp.sin(angles)])


def inverse_freq(dim_count):
    return rope_theta ** (-jnp.arange(0, dim_count, 2, dtype=jnp.float32) / dim_count)


def rotary_angles(height_pos, width_pos):
    still_dims = HD // 8
    axis_dims = (HD - still_dims) // 2
    return jnp.concatenate(
        [
            jnp.zeros((height_pos.shape[0], still_dims // 2), jnp.float32),
            height_pos[:, None] * inverse_freq(axis_dims)[None],
            width_pos[:, None] * inverse_freq(axis_dims)[None],
        ],
        axis=1,
    )


def rotate(vectors, angles):
    paired_dims = vectors.reshape(vectors.shape[:-1] + (HD // 2, 2))
    cosine_table = jnp.cos(angles)[:, None, :]
    sine_table = jnp.sin(angles)[:, None, :]
    first_part = paired_dims[..., 0]
    second_part = paired_dims[..., 1]
    turned = jnp.stack(
        [
            first_part * cosine_table - second_part * sine_table,
            first_part * sine_table + second_part * cosine_table,
        ],
        axis=-1,
    )
    return turned.reshape(vectors.shape)


def head_norm(vectors, gain_vector):
    return (
        vectors
        * lax.rsqrt(jnp.mean(vectors * vectors, axis=-1, keepdims=True) + epsilon)
        * gain_vector
    )


def input_folder(source, pieces):
    width_rows = pieces[0].shape[0]
    first_total = jnp.dot(
        source, pieces[0].reshape(width_rows, -1), preferred_element_type=jnp.float32
    )
    second_total = jnp.dot(source, pieces[1], preferred_element_type=jnp.float32)
    return (first_total, second_total)


def output_folder(attended, activated, pieces):
    block_cols = jnp.dot(attended, pieces[0], preferred_element_type=jnp.float32)
    block_cols = block_cols + jnp.dot(activated, pieces[1], preferred_element_type=jnp.float32)
    return block_cols


def shards(
    text_tokens,
    image_tokens,
    pooled_vector,
    mod_weight,
    qkv_weight,
    up_weight,
    query_gain,
    key_gain,
    attn_weight,
    down_weight,
    lengths,
    timestep,
):
    seq_pos = lax.axis_index("seq")
    cfg_pos = lax.axis_index("cfg")
    prompts = image_tokens.shape[0]
    image_rows = image_tokens.shape[1]
    text_rows = text_tokens.shape[2]
    local_len = text_rows + image_rows
    dim_local = image_tokens.shape[2]
    dim_seq = pooled_vector.shape[1]
    heads_local = qkv_weight.shape[2]
    row_count = prompts * local_len
    sigma_now, step_size = plan(timestep)
    embedded = lax.dynamic_slice_in_dim(time_embedding(sigma_now, D), seq_pos * dim_seq, dim_seq)
    cond_vec = jax.nn.silu(pooled_vector[0] + embedded).astype(jnp.bfloat16)[None]
    mod_terms = jnp.dot(
        cond_vec, mod_weight.reshape(dim_seq, 3 * dim_local), preferred_element_type=jnp.float32
    )
    modulation = lax.psum(mod_terms.reshape(3, dim_local), "seq")
    local_rows = jnp.concatenate([text_tokens[0], image_tokens], axis=1)
    hidden = local_rows.astype(jnp.float32)
    totals, squares = lax.psum(
        (jnp.sum(hidden, axis=-1), jnp.sum(hidden * hidden, axis=-1)), "wblk"
    )
    average = (totals / D)[..., None]
    variance = (squares / D)[..., None] - average * average
    normed = (
        (hidden - average) * lax.rsqrt(variance + epsilon) * (1.0 + modulation[1]) + modulation[0]
    ).astype(jnp.bfloat16)
    gathered = lax.all_gather(normed, "wblk", axis=2, tiled=True)
    token_rows = gathered.reshape(row_count, D)
    projected, mlp_units = input_folder(
        token_rows,
        (
            lax.all_gather(qkv_weight, "seq", axis=0, tiled=True),
            lax.all_gather(up_weight, "seq", axis=0, tiled=True),
        ),
    )
    projected = projected.reshape(prompts, local_len, 3, heads_local, HD)
    image_index = seq_pos * image_rows + jnp.arange(image_rows, dtype=jnp.int32)
    height_pos = jnp.concatenate(
        [jnp.zeros((text_rows,), jnp.float32), (image_index // GRID).astype(jnp.float32)]
    )
    width_pos = jnp.concatenate(
        [jnp.zeros((text_rows,), jnp.float32), (image_index % GRID).astype(jnp.float32)]
    )
    angles = rotary_angles(height_pos, width_pos)
    queries = rotate(head_norm(projected[:, :, 0], query_gain), angles).astype(jnp.bfloat16)
    key_rows = rotate(head_norm(projected[:, :, 1], key_gain), angles).astype(jnp.bfloat16)
    values = projected[:, :, 2].astype(jnp.bfloat16)
    scale_factor = HD ** (-0.5)
    running_max = jnp.full((prompts, heads_local, local_len), -1e30, jnp.float32)
    key_piece = lax.all_gather(key_rows, "seq", axis=1, tiled=True)
    value_piece = lax.all_gather(values, "seq", axis=1, tiled=True)
    width_keys = key_piece.shape[1]
    where_global = jnp.arange(width_keys, dtype=jnp.int32)
    shard_index = where_global // local_len
    within = where_global % local_len
    text_index = shard_index * text_rows + within
    key_live = (within >= text_rows)[None, :] | (text_index[None, :] < lengths[:, None])
    scores = (
        jnp.einsum("pqhd,pkhd->phqk", queries, key_piece, preferred_element_type=jnp.float32)
        * scale_factor
    )
    scores = jnp.where(key_live[:, None, None, :], scores, -1e30)
    new_max = jnp.maximum(running_max, jnp.max(scores, axis=-1))
    weights = jnp.exp(scores - new_max[..., None])
    denominator = jnp.sum(weights, axis=-1)
    numerator = jnp.einsum(
        "phqk,pkhd->phqd",
        weights.astype(jnp.bfloat16),
        value_piece,
        preferred_element_type=jnp.float32,
    )
    running_max, denominator, numerator = (new_max, denominator, numerator)
    attended = (numerator / denominator[..., None]).astype(jnp.bfloat16)
    attended = attended.transpose(0, 2, 1, 3).reshape(row_count, heads_local * HD)
    activated = jax.nn.gelu(mlp_units, approximate=True).astype(jnp.bfloat16)
    branch_terms = output_folder(
        attended,
        activated,
        (
            lax.all_gather(attn_weight, "seq", axis=1, tiled=True),
            lax.all_gather(down_weight, "seq", axis=1, tiled=True),
        ),
    )
    branch = lax.psum_scatter(
        branch_terms.reshape(prompts, local_len, D).astype(jnp.bfloat16),
        "wblk",
        scatter_dimension=2,
        tiled=True,
    ).astype(jnp.float32)
    layer_out = hidden + modulation[2] * branch
    text_out = layer_out[:, :text_rows].astype(jnp.bfloat16)[None]
    image_out = layer_out[:, text_rows:]
    paired = lax.all_to_all(
        image_out[:, None].astype(jnp.bfloat16), "cfg", split_axis=0, concat_axis=1, tiled=True
    ).astype(jnp.float32)
    velocity = paired[:, 1] + guidance * (paired[:, 0] - paired[:, 1])
    own_prompts = prompts // 2
    latent = lax.dynamic_slice_in_dim(image_tokens, cfg_pos * own_prompts, own_prompts, 0).astype(
        jnp.float32
    )
    new_image = latent + step_size * velocity
    return (text_out, velocity, new_image)


def solution(mesh):
    in_specs = (
        P("cfg", None, "seq", "wblk"),
        P(None, "seq", "wblk"),
        P("cfg", "seq"),
        P("seq", None, "wblk"),
        P("seq", None, "wblk", None),
        P("seq", "wblk"),
        P(),
        P(),
        P("wblk", "seq"),
        P("wblk", "seq"),
        P(),
        P(),
    )
    out_specs = (P("cfg", None, "seq", "wblk"), P("cfg", "seq", "wblk"), P("cfg", "seq", "wblk"))
    return jax.shard_map(shards, mesh=mesh, in_specs=in_specs, out_specs=out_specs, check_vma=False)
```

profile of v0, /device:TPU:0, one launch (start us, length us, event | category | flops | bytes accessed | tf_op | source)
XLA Modules:
  0.0 1203.3 jit_solution(4073631650355688277)
XLA Ops:
  7.2 0.0 all-gather.11.cloned.1.call-start
  7.2 0.7 all-gather.11.cloned.1.call-update
  7.9 0.0 all-gather.9.cloned.1.call-start
  8.6 0.7 reduce.2
  9.4 0.1 fusion.53
  9.4 0.1 multiply_convert_fusion
  9.6 6.2 copy.27
  15.8 3.0 fusion.34
  18.8 24.9 %psum.21 = f32[3,768]{1,0:T(4,128)} all-reduce(f32[3,768]{1,0:T(4,128)S(1)} %bitcast.95), channel_id=1, replica_groups=mesh['cfg'=2,'seq'=4,'wblk'=4] {'seq'}, use_global_device_ids=true, to_apply=%region_0.1 | all-reduce | flops 2304 | bytes 18432 | tf_op jit(solution)/shard_map/psum | solution.py:122
  43.7 1.8 convert_reduce_fusion
  45.5 11.6 all-reduce.2
  57.1 1.4 slice_reduce_fusion.1
  58.6 0.7 broadcast_multiply_fusion.2
  59.3 2.7 fusion.21
  62.1 0.0 all-gather.17.cloned.1.call-start
  62.1 0.7 all-gather.17.cloned.1.call-update
  62.8 0.0 all-gather.13.cloned.1.call-start
  62.8 0.1 mul.305
  63.0 0.1 mul.324
  63.2 0.1 broadcast_multiply_fusion.1
  63.3 1.0 fusion.44
  64.3 115.2 %all-gather.11.cloned.1.call-done = bf16[3072,3,4,128]{3,2,1,0:T(4,128)(2,1)} async-done(((bf16[768,3,4,128]{3,2,1,0:T(4,128)(2,1)}), bf16[3072,3,4,128]{3,2,1,0:T(4,128)(2,1)}) %all-gather.11.cloned.1.call-update) | async-done | bytes 9437200 | tf_op jit(solution)/shard_map/all_gather | solution.py:138
  179.5 15.9 %copy.39 = bf16[3072,3,4,128]{0,3,2,1:T(8,128)(2,1)} copy(bf16[3072,3,4,128]{3,2,1,0:T(4,128)(2,1)} %all-gather.11.cloned.1.call-done) | data formatting | bytes 18874368 | tf_op jit(solution)/shard_map/reshape | solution.py:80
  195.4 74.9 %all-gather.9.cloned.1.call-done = bf16[2,1152,3072]{2,1,0:T(8,128)(2,1)} async-done(((bf16[2,1152,768]{2,1,0:T(8,128)(2,1)}), bf16[2,1152,3072]{2,1,0:T(8,128)(2,1)}) %all-gather.9.cloned.1.call-update) | async-done | bytes 14155792 | tf_op jit(solution)/shard_map/all_gather | solution.py:133
  270.4 32.0 %fusion.14 = f32[2,1152,3,4,128]{1,4,3,2,0:T(8,128)} fusion(bf16[2,1152,3072]{2,1,0:T(8,128)(2,1)} %all-gather.9.cloned.1.call-done, bf16[3072,3,4,128]{0,3,2,1:T(8,128)(2,1)} %copy.39), kind=kOutput, calls=%fused_computation.17 | convolution fusion | flops 21743271936 | bytes 37748736 | tf_op jit(solution)/shard_map/dot_general | solution.py:79
  302.4 5.6 multiply_reduce_fusion.1
  307.9 3.0 copy.40
  311.0 3.0 copy.41
  314.1 0.9 multiply_multiply_fusion.2
  315.0 0.9 multiply_multiply_fusion.1
  316.0 3.5 subtract_convert_fusion.1
  319.5 1.5 pad_maximum_fusion.2
  321.1 3.6 copy.31
  324.6 0.0 all-gather.13.cloned.1.call-update
  324.7 0.0 all-gather.21.cloned.1.call-start
  324.7 4.1 slice.102
  328.9 0.0 all-gather.15.cloned.1.call-start
  328.9 0.5 all-gather.15.cloned.1.call-update
  329.5 0.0 all-gather.19.cloned.1.call-start
  329.5 0.7 all-gather.19.cloned.1.call-update
  330.2 0.0 reduce-scatter.2.cloned.1.call-start
  330.3 0.1 compare_or_fusion
  330.4 3.2 pad_maximum_fusion.1
  333.6 105.1 %all-gather.17.cloned.1.call-done = bf16[3072,1536]{1,0:T(8,128)(2,1)} async-done(((bf16[768,1536]{1,0:T(8,128)(2,1)}), bf16[3072,1536]{1,0:T(8,128)(2,1)}) %all-gather.17.cloned.1.call-update) | async-done | bytes 9437200 | tf_op jit(solution)/shard_map/all_gather | solution.py:139
  438.7 30.9 %fusion.88 = bf16[2304,1536]{1,0:T(8,128)(2,1)} fusion(bf16[2304,3072]{1,0:T(8,128)(2,1)} %bitcast.96, bf16[3072,1536]{1,0:T(8,128)(2,1)} %all-gather.17.cloned.1.call-done), kind=kOutput, calls=%fused_computation.16.clone.clone.1 | convolution fusion | flops 21775122432 | bytes 30670848 | tf_op jit(solution)/shard_map/dot_general | solution.py:82
  469.6 136.1 %all-gather.13.cloned.1.call-done = bf16[2,4608,4,128]{3,1,2,0:T(8,128)(2,1)} async-done(((bf16[2,1152,4,128]{3,1,2,0:T(8,128)(2,1)}), bf16[2,4608,4,128]{3,1,2,0:T(8,128)(2,1)}) %all-gather.13.cloned.1.call-update) | async-done | bytes 9437200 | tf_op jit(solution)/shard_map/all_gather | solution.py:156
  605.7 63.5 %fusion.70 = (f32[2,4,1152]{2,1,0:T(4,128)S(1)}, f32[2,4,1152,4608]{3,2,1,0:T(8,128)}) fusion(bf16[2,4608,4,128]{3,1,2,0:T(8,128)(2,1)} %all-gather.13.cloned.1.call-done, bf16[2,1152,4,128]{1,2,3,0:T(4,128)(2,1)S(1)} %bitcast.87, pred[2,4608]{1,0:T(4,128)(4,1)S(1)} %compare_or_fusion), kind=kOutput, calls=%fused_computation.120 | convolution fusion | flops 10999028736 | bytes 181711872 | tf_op jit(solution)/shard_map/pqhd,pkhd->phqk/dot_general | solution.py:165
  669.3 51.4 %fusion.1 = f32[2,4,1152]{2,1,0:T(4,128)S(1)} fusion(f32[2,4,1152,4608]{3,2,1,0:T(8,128)} %get-tuple-element.29, f32[2,4,1152]{2,1,0:T(4,128)S(1)} %broadcast_maximum_fusion), kind=kLoop, calls=%fused_computation.3 | loop fusion | flops 84925440 | bytes 169943040 | tf_op jit(solution)/shard_map/reduce_sum | solution.py:171
  720.6 52.1 %all-gather.21.cloned.1.call-done = bf16[2,4608,1,4,128]{1,4,3,2,0:T(8,128)(2,1)} async-done(((bf16[2,1152,1,4,128]{1,4,3,2,0:T(8,128)(2,1)}), bf16[2,4608,1,4,128]{1,4,3,2,0:T(8,128)(2,1)}) %all-gather.21.cloned.1.call-update) | async-done | bytes 9437200 | tf_op jit(solution)/shard_map/all_gather | solution.py:157
  772.8 56.5 %fusion.29 = bf16[2,1152,4,128]{3,1,2,0:T(8,128)(2,1)S(1)} fusion(bf16[2,4608,1,4,128]{1,4,3,2,0:T(8,128)(2,1)} %all-gather.21.cloned.1.call-done, f32[2,4,1152,4608]{3,2,1,0:T(8,128)} %get-tuple-element.29, f32[2,4,1152]{2,1,0:T(4,128)S(1)} %broadcast_maximum_fusion, f32[2,1152,4]{1,2,0:T(4,128)S(1)} %bitcast.93), kind=kOutput, calls=%fused_computation.37 | convolution fusion | flops 10958929920 | bytes 181739520 | tf_op jit(solution)/shard_map/phqk,pkhd->phqd/dot_general | solution.py:172
  829.2 6.7 copy.34
  836.0 17.2 %fusion.39 = f32[2304,3072]{1,0:T(8,128)} fusion(bf16[512,3072]{1,0:T(8,128)(2,1)} %all-gather.15.cloned.1.call-done, bf16[288,8,4,128]{3,2,1,0:T(4,128)(2,1)} %bitcast.94), kind=kOutput, calls=%fused_computation.53 | convolution fusion | flops 7247757312 | bytes 33816576 | tf_op jit(solution)/shard_map/dot_general | solution.py:87
  853.1 149.8 %all-gather.19.cloned.1.call-done = bf16[1536,3072]{1,0:T(8,128)(2,1)} async-done(((bf16[1536,768]{1,0:T(8,128)(2,1)}), bf16[1536,3072]{1,0:T(8,128)(2,1)}) %all-gather.19.cloned.1.call-update) | async-done | bytes 9437200 | tf_op jit(solution)/shard_map/all_gather | solution.py:187
  1002.9 31.7 %add_convert_fusion = bf16[2304,3072]{1,0:T(8,128)(2,1)} fusion(f32[2304,3072]{1,0:T(8,128)} %fusion.39, bf16[1536,3072]{1,0:T(8,128)(2,1)} %all-gather.19.cloned.1.call-done, bf16[2304,1536]{1,0:T(8,128)(2,1)} %fusion.88), kind=kOutput, calls=%fused_computation.7 | convolution fusion | flops 21757427712 | bytes 58982400 | tf_op jit(solution)/shard_map/dot_general | solution.py:88
  1034.7 0.0 reduce-scatter.2.cloned.1.call-update
  1034.7 107.8 %reduce-scatter.2.cloned.1.call-done = bf16[2,1152,768]{2,1,0:T(8,128)(2,1)} async-done(((bf16[2,1152,3072]{2,1,0:T(8,128)(2,1)}), bf16[2,1152,768]{2,1,0:T(8,128)(2,1)}) %reduce-scatter.2.cloned.1.call-update) | async-done | bytes 3538960 | tf_op jit(solution)/shard_map/reduce_scatter | solution.py:190
  1142.5 2.6 fusion.23
  1145.2 1.7 copy-done.2
  1146.9 1.9 slice_bitcast_fusion.2
  1148.8 5.2 all-to-all-start
  1154.1 1.8 slice_bitcast_fusion.3
  1155.8 34.6 %all-to-all-done = bf16[2,1,1024,768]{3,2,1,0:T(8,128)(2,1)} async-done(((bf16[2,1,1024,768]{3,2,1,0:T(8,128)(2,1)}), bf16[2,1,1024,768]{3,2,1,0:T(8,128)(2,1)}, u32[]{:S(2)}, u32[]{:S(2)}) %all-to-all-start) | async-done | bytes 3145760 | tf_op jit(solution)/shard_map/all_to_all | solution.py:199
  1190.4 2.4 bitcast_convert_fusion
  1192.8 3.4 multiply_add_fusion
  (33 shorter events, 0.2 us)
Async XLA Ops:
  7.2 172.3 %all-gather.11.cloned.1.call-start = ((), (), s32[]{:S(2)}) async-start(), calls=%async_computation.3 | async-start | bytes 11796480 | tf_op jit(solution)/shard_map/all_gather | solution.py:138
  7.9 262.5 %all-gather.9.cloned.1.call-start = ((), (), s32[]{:S(2)}) async-start(), calls=%async_computation.2 | async-start | bytes 17694720 | tf_op jit(solution)/shard_map/all_gather | solution.py:133
  9.5 34.1 %copy-start = (bf16[2,1024,768]{2,1,0:T(8,128)(2,1)S(1)}, bf16[2,1024,768]{2,1,0:T(8,128)(2,1)}, u32[]{:S(2)}) copy-start(bf16[2,1024,768]{2,1,0:T(8,128)(2,1)} %param.13) | copy-start | bytes 9437188
  9.5 34.1 %copy-start.3 = (bf16[1,2,128,768]{3,2,1,0:T(8,128)(2,1)S(1)}, bf16[1,2,128,768]{3,2,1,0:T(8,128)(2,1)}, u32[]{:S(2)}) copy-start(bf16[1,2,128,768]{3,2,1,0:T(8,128)(2,1)} %param.12) | copy-start | bytes 1179652
  62.0 0.8 copy-start.6
  62.0 1.0 copy-start.7
  62.1 376.7 %all-gather.17.cloned.1.call-start = ((), (), s32[]{:S(2)}) async-start(), calls=%async_computation.6 | async-start | bytes 11796480 | tf_op jit(solution)/shard_map/all_gather | solution.py:139
  62.8 542.9 %all-gather.13.cloned.1.call-start = ((), (), s32[]{:S(2)}) async-start(), calls=%async_computation.4 | async-start | bytes 11796480 | tf_op jit(solution)/shard_map/all_gather | solution.py:156
  324.7 5.6 copy-start.8
  324.7 448.1 %all-gather.21.cloned.1.call-start = ((), (), s32[]{:S(2)}) async-start(), calls=%async_computation.9 | async-start | bytes 11796480 | tf_op jit(solution)/shard_map/all_gather | solution.py:157
  328.9 507.1 %all-gather.15.cloned.1.call-start = ((), (), s32[]{:S(2)}) async-start(), calls=%async_computation.5 | async-start | bytes 3932160 | tf_op jit(solution)/shard_map/all_gather | solution.py:186
  329.5 673.5 %all-gather.19.cloned.1.call-start = ((), (), s32[]{:S(2)}) async-start(), calls=%async_computation.7 | async-start | bytes 11796480 | tf_op jit(solution)/shard_map/all_gather | solution.py:187
  330.2 812.3 %reduce-scatter.2.cloned.1.call-start = ((), (), s32[]{:S(2)}) async-start(), calls=%async_computation.8 | async-start | bytes 17694720 | tf_op jit(solution)/shard_map/reduce_scatter | solution.py:190
  1034.7 107.9 %copy-start.1 = (bf16[2,1024,768]{2,1,0:T(8,128)(2,1)S(1)}, bf16[2,1024,768]{2,1,0:T(8,128)(2,1)}, u32[]{:S(2)}) copy-start(bf16[2,1024,768]{2,1,0:T(8,128)(2,1)} %param.13) | copy-start | bytes 9437188
  1034.7 107.9 %copy-start.4 = (bf16[1,2,128,768]{3,2,1,0:T(8,128)(2,1)S(1)}, bf16[1,2,128,768]{3,2,1,0:T(8,128)(2,1)}, u32[]{:S(2)}) copy-start(bf16[1,2,128,768]{3,2,1,0:T(8,128)(2,1)} %param.12) | copy-start | bytes 1179652
  1034.7 107.9 %copy-start.5 = (f32[768]{0:T(1024)S(1)}, f32[768]{0:T(1024)}, u32[]{:S(2)}) copy-start(f32[768]{0:T(1024)} %get-tuple-element.7) | copy-start | bytes 9220
  1145.2 1.8 copy-start.2
  1148.8 41.6 %all-to-all-start = ((bf16[2,1,1024,768]{3,2,1,0:T(8,128)(2,1)}), bf16[2,1,1024,768]{3,2,1,0:T(8,128)(2,1)}, u32[]{:S(2)}, u32[]{:S(2)}) async-start(bf16[2,1,1024,768]{3,2,1,0:T(8,128)(2,1)} %slice_bitcast_fusion.2), calls=%async_computation.1 | async-start | bytes 6291456 | tf_op jit(solution)/shard_map/all_to_all | solution.py:199
Sparse Core Ops, SparseCore 0:
  9.6 169.8 all-gather.10
  181.0 89.2 all-gather.8
  271.9 166.7 all-gather.16
  440.7 164.9 all-gather.12
  607.8 164.9 all-gather.20
  774.2 61.6 all-gather.14
  837.4 165.4 all-gather.18
  1034.8 107.6 reduce-scatter.1
where the time goes:
time: 1210 us; the launch traced here: 1200 us
  waiting for transfers between devices  778 us (64%)
  matrix products  235 us (19%)
  other arithmetic  84.3 us (7%)
  local copies, waits for them, and re-layouts  48.4 us (4%)
  blocking collectives  36.5 us (3%)
  between operations  15.4 us (1%)
    all_gather x1, waiting for transfers between devices, shards(): lax.all_gather(down_weight, 'seq', axis=1, tiled=True)  150 us
    all_gather x1, waiting for transfers between devices, shards(): key_piece = lax.all_gather(key_rows, 'seq', axis=1, tiled=True)  136 us
    all_gather x1, waiting for transfers between devices, shards(): lax.all_gather(qkv_weight, 'seq', axis=0, tiled=True)  115 us
    reduce_scatter x1, waiting for transfers between devices, shards(): lax.psum_scatter(branch_terms.reshape(prompts, local_len, D).astype(jnp.b...  108 us
    all_gather x1, waiting for transfers between devices, shards(): lax.all_gather(up_weight, 'seq', axis=0, tiled=True)  105 us
    all_gather x1, waiting for transfers between devices, shards(): gathered = lax.all_gather(normed, 'wblk', axis=2, tiled=True)  74.9 us
    dot_general x1, matrix products, shards(): jnp.einsum('pqhd,pkhd->phqk', queries, key_piece, preferred_element_type=...  63.5 us
    dot_general x1, matrix products, shards(): jnp.einsum('phqk,pkhd->phqd', weights.astype(jnp.bfloat16), value_piece,...  56.5 us
  transfers between devices with their start and end apart: 9, of which 8 were waited for; matrix products, arithmetic and copies ran while one was open for 27% of the time, Pallas kernels for 0%

commit v1 on v0

v1 whole, which is shorter than its diff:
```python
import functools
import math

import jax
import jax.numpy as jnp
from jax import lax
from jax.experimental import pallas as pl
from jax.experimental.pallas import tpu as pltpu
from jax.sharding import PartitionSpec as P

D = 3072
HD = 128
GRID = 64
STEPS = 28

epsilon = 1e-06
guidance = 3.5
time_shift = 3.0
rope_theta = 10000.0
VMEM = 60 * 1024 * 1024


def plan(timestep):
    step_index = timestep[0].astype(jnp.float32)
    time_now = 1.0 - step_index / STEPS
    time_next = 1.0 - (step_index + 1.0) / STEPS
    sigma_now = time_shift * time_now / (1.0 + (time_shift - 1.0) * time_now)
    sigma_next = time_shift * time_next / (1.0 + (time_shift - 1.0) * time_next)
    return (sigma_now, sigma_next - sigma_now)


def time_embedding(sigma_now, dim_count):
    halfwidth = dim_count // 2
    frequency = jnp.exp(-math.log(10000.0) * jnp.arange(halfwidth, dtype=jnp.float32) / halfwidth)
    angles = 1000.0 * sigma_now * frequency
    return jnp.concatenate([jnp.cos(angles), jnp.sin(angles)])


def inverse_freq(dim_count):
    return rope_theta ** (-jnp.arange(0, dim_count, 2, dtype=jnp.float32) / dim_count)


def rotary_angles(height_pos, width_pos):
    still_dims = HD // 8
    axis_dims = (HD - still_dims) // 2
    return jnp.concatenate(
        [
            jnp.zeros((height_pos.shape[0], still_dims // 2), jnp.float32),
            height_pos[:, None] * inverse_freq(axis_dims)[None],
            width_pos[:, None] * inverse_freq(axis_dims)[None],
        ],
        axis=1,
    )


def largest_block(rows, limit, unit=16):
    best = rows
    for size in range(unit, min(rows, limit) + 1, unit):
        if rows % size == 0:
            best = size
    return best


def qkv_body(heads, x_ref, w_ref, cos_ref, sin_ref, gain_ref, out_ref):
    result = jnp.dot(x_ref[0, 0], w_ref[...], preferred_element_type=jnp.float32)
    cosine = cos_ref[...]
    sine = sin_ref[...]
    even = lax.broadcasted_iota(jnp.int32, cosine.shape, 1) % 2 == 0
    for head in range(heads):
        for kind in range(3):
            start = (kind * heads + head) * HD
            part = result[:, start : start + HD]
            if kind < 2:
                mean_sq = jnp.mean(part * part, axis=-1, keepdims=True)
                part = part * lax.rsqrt(mean_sq + epsilon) * gain_ref[kind : kind + 1]
                other = jnp.where(even, pltpu.roll(part, HD - 1, 1), pltpu.roll(part, 1, 1))
                part = part * cosine + other * sine
            out_ref[0, 0, head, kind] = part.astype(jnp.bfloat16)


def project_qkv(normed, weight, cosine, sine, gains, heads):
    halves, prompts, rows, _ = normed.shape
    block = largest_block(rows, 384)
    grid = (halves, prompts, rows // block)
    return pl.pallas_call(
        functools.partial(qkv_body, heads),
        grid=grid,
        in_specs=[
            pl.BlockSpec((1, 1, block, D), lambda c, p, i: (c, p, i, 0)),
            pl.BlockSpec((D, 3 * heads * HD), lambda c, p, i: (0, 0)),
            pl.BlockSpec((block, HD), lambda c, p, i: (i, 0)),
            pl.BlockSpec((block, HD), lambda c, p, i: (i, 0)),
            pl.BlockSpec((2, HD), lambda c, p, i: (0, 0)),
        ],
        out_specs=pl.BlockSpec((1, 1, heads, 3, block, HD), lambda c, p, i: (c, p, 0, 0, i, 0)),
        out_shape=jax.ShapeDtypeStruct((halves, prompts, heads, 3, rows, HD), jnp.bfloat16),
        compiler_params=pltpu.CompilerParams(vmem_limit_bytes=VMEM),
        cost_estimate=pl.CostEstimate(
            flops=2 * halves * prompts * rows * D * 3 * heads * HD,
            bytes_accessed=2 * halves * prompts * rows * D + 6 * D * heads * HD,
            transcendentals=0,
        ),
        name="project_qkv",
    )(normed, weight, cosine, sine, gains)


def attention_body(shards_of, rows, text_rows, live_ref, q_ref, k_ref, v_ref, out_ref):
    unit = pl.program_id(0)
    live = live_ref[unit]
    factor = HD ** (-0.5) * math.log2(math.e)
    queries = q_ref[0, 0, 0]
    image_rows = rows - text_rows
    first = image_rows // HD * HD

    def score(shard):
        part = lax.dot_general(
            queries, k_ref[shard, 0, 0], (((1,), (1,)), ((), ())), preferred_element_type=jnp.float32
        )
        tail = part[:, first:]
        column = lax.broadcasted_iota(jnp.int32, tail.shape, 1) + (first - image_rows)
        tail = jnp.where((column < 0) | (column + shard * text_rows < live), tail, -1e30)
        if first == 0:
            return tail
        return jnp.concatenate([part[:, :first], tail], axis=1)

    top = None
    following = score(0)
    for shard in range(shards_of):
        scores = following
        if shard + 1 < shards_of:
            following = score(shard + 1)
        highest = jnp.max(scores, axis=-1, keepdims=True)
        if top is not None:
            highest = jnp.maximum(top, highest)
        weights = jnp.exp2((scores - highest) * factor)
        total = jnp.sum(weights, axis=-1, keepdims=True)
        mixed = jnp.dot(
            weights.astype(jnp.bfloat16), v_ref[shard, 0, 0], preferred_element_type=jnp.float32
        )
        if top is not None:
            shrink = jnp.exp2((top - highest) * factor)
            total = total + denominator * shrink
            mixed = mixed + numerator * shrink
        top, denominator, numerator = highest, total, mixed
    out_ref[0, 0] = (numerator / denominator).astype(jnp.bfloat16)


def attention(live, queries, keys_values, text_rows):
    query_shards, units, _, rows, _ = queries.shape
    shards_of = keys_values.shape[0]
    block = largest_block(rows, 384)
    return pl.pallas_call(
        functools.partial(attention_body, shards_of, rows, text_rows),
        grid_spec=pltpu.PrefetchScalarGridSpec(
            num_scalar_prefetch=1,
            grid=(units, query_shards, rows // block),
            in_specs=[
                pl.BlockSpec((1, 1, 1, block, HD), lambda u, s, i, live: (s, u, 0, i, 0)),
                pl.BlockSpec((shards_of, 1, 1, rows, HD), lambda u, s, i, live: (0, u, 1, 0, 0)),
                pl.BlockSpec((shards_of, 1, 1, rows, HD), lambda u, s, i, live: (0, u, 2, 0, 0)),
            ],
            out_specs=pl.BlockSpec((1, 1, block, HD), lambda u, s, i, live: (s, u, i, 0)),
        ),
        out_shape=jax.ShapeDtypeStruct((query_shards, units, rows, HD), jnp.bfloat16),
        compiler_params=pltpu.CompilerParams(vmem_limit_bytes=VMEM),
        cost_estimate=pl.CostEstimate(
            flops=4 * query_shards * units * rows * shards_of * rows * HD,
            bytes_accessed=8 * query_shards * units * rows * HD,
            transcendentals=query_shards * units * rows * shards_of * rows,
        ),
        name="attention",
    )(live, queries, keys_values, keys_values)


def guided_body(heads, col_blocks, att_ref, act_ref, w_ref, gate_ref, out_ref):
    width = w_ref.shape[2]
    block = out_ref.shape[1]
    stacked = []
    for half in range(2):
        pieces = [att_ref[half, 0, head] for head in range(heads)] + [act_ref[half, 0]]
        stacked.append(jnp.concatenate(pieces, axis=1))
    terms = jnp.concatenate(stacked, axis=0)
    for col in range(col_blocks):
        part = jnp.dot(terms, w_ref[col], preferred_element_type=jnp.float32)
        span = slice(col * width, (col + 1) * width)
        guided = part[:block] * (guidance * gate_ref[0:1, span])
        guided = guided - part[block:] * ((guidance - 1.0) * gate_ref[1:2, span])
        out_ref[0, :, span] = guided.astype(jnp.bfloat16)


def guided_terms(attended, activated, weight, gate, image_rows):
    halves, prompts, heads, rows, _ = attended.shape
    units = activated.shape[3]
    col_blocks, depth, width = weight.shape
    block = largest_block(image_rows, 256)
    return pl.pallas_call(
        functools.partial(guided_body, heads, col_blocks),
        grid=(prompts, image_rows // block),
        in_specs=[
            pl.BlockSpec((2, 1, heads, block, HD), lambda p, i: (0, p, 0, i, 0)),
            pl.BlockSpec((2, 1, block, units), lambda p, i: (0, p, i, 0)),
            pl.BlockSpec((col_blocks, depth, width), lambda p, i: (0, 0, 0)),
            pl.BlockSpec((2, D), lambda p, i: (0, 0)),
        ],
        out_specs=pl.BlockSpec((1, block, D), lambda p, i: (p, i, 0)),
        out_shape=jax.ShapeDtypeStruct((prompts, image_rows, D), jnp.bfloat16),
        compiler_params=pltpu.CompilerParams(vmem_limit_bytes=VMEM),
        cost_estimate=pl.CostEstimate(
            flops=4 * prompts * image_rows * depth * D,
            bytes_accessed=2 * (prompts * image_rows * (2 * depth + D) + depth * D),
            transcendentals=0,
        ),
        name="guided_terms",
    )(attended, activated, weight, gate)


CORE_SWAP = [(0, 1), (1, 0), (2, 3), (3, 2)]
CHIP_SWAP = [(0, 2), (2, 0), (1, 3), (3, 1)]


def gather_features(block, wblk_pos, wblk_size):
    if wblk_size != 4:
        return lax.all_gather(block, "wblk", axis=block.ndim - 1, tiled=True)
    far = lax.ppermute(block, "wblk", CHIP_SWAP)
    near = lax.ppermute(block, "wblk", CORE_SWAP)
    far_near = lax.ppermute(far, "wblk", CORE_SWAP)
    odd = wblk_pos % 2 == 1
    here = jnp.where(odd, jnp.concatenate([near, block], -1), jnp.concatenate([block, near], -1))
    there = jnp.where(odd, jnp.concatenate([far_near, far], -1), jnp.concatenate([far, far_near], -1))
    upper = wblk_pos >= 2
    return jnp.where(upper, jnp.concatenate([there, here], -1), jnp.concatenate([here, there], -1))


def scatter_features(terms, wblk_pos, wblk_size):
    last = terms.ndim - 1
    if wblk_size != 4:
        summed = lax.psum_scatter(terms, "wblk", scatter_dimension=last, tiled=True)
        return summed.astype(jnp.float32)
    width = terms.shape[last] // 4

    def block(array, index):
        return lax.dynamic_slice_in_dim(array, index * width, width, last)

    core_mate = wblk_pos + 1 - 2 * (wblk_pos % 2)
    chip_mate = (wblk_pos + 2) % 4
    both_mate = (core_mate + 2) % 4
    far_part = block(terms, chip_mate).astype(jnp.float32) + lax.ppermute(
        block(terms, both_mate), "wblk", CORE_SWAP
    ).astype(jnp.float32)
    far_sum = lax.ppermute(far_part.astype(jnp.bfloat16), "wblk", CHIP_SWAP).astype(jnp.float32)
    near_part = lax.ppermute(block(terms, core_mate), "wblk", CORE_SWAP).astype(jnp.float32)
    return block(terms, wblk_pos).astype(jnp.float32) + near_part + far_sum


def shards(
    cfg_size,
    seq_size,
    wblk_size,
    text_tokens,
    image_tokens,
    pooled_vector,
    mod_weight,
    qkv_weight,
    up_weight,
    query_gain,
    key_gain,
    attn_weight,
    down_weight,
    lengths,
    timestep,
):
    seq_pos = lax.axis_index("seq")
    cfg_pos = lax.axis_index("cfg")
    wblk_pos = lax.axis_index("wblk")
    prompts, image_rows, dim_local = image_tokens.shape
    text_rows = text_tokens.shape[2]
    local_len = text_rows + image_rows
    dim_seq = pooled_vector.shape[1]
    heads = qkv_weight.shape[2] // cfg_size
    units = up_weight.shape[1] // cfg_size

    qkv_part = lax.dynamic_slice_in_dim(qkv_weight, cfg_pos * heads, heads, 2)
    qkv_part = qkv_part.reshape(dim_seq, 3 * heads * HD)
    qkv_full = lax.all_gather(qkv_part, "seq", axis=0, tiled=True)
    up_part = lax.dynamic_slice_in_dim(up_weight, cfg_pos * units, units, 1)
    up_full = lax.all_gather(up_part, "seq", axis=0, tiled=True)
    out_part = jnp.concatenate(
        [
            lax.dynamic_slice_in_dim(attn_weight, cfg_pos * heads * HD, heads * HD, 0),
            lax.dynamic_slice_in_dim(down_weight, cfg_pos * units, units, 0),
        ],
        axis=0,
    )
    out_full = lax.all_gather(out_part, "seq", axis=0)

    text_other = lax.ppermute(text_tokens[0], "cfg", [(0, 1), (1, 0)])
    text_both = jnp.where(
        cfg_pos == 0, jnp.stack([text_tokens[0], text_other]), jnp.stack([text_other, text_tokens[0]])
    )
    image_full = gather_features(image_tokens, wblk_pos, wblk_size)
    text_full = gather_features(text_both, wblk_pos, wblk_size)

    sigma_now, step_size = plan(timestep)
    embedded = lax.dynamic_slice_in_dim(time_embedding(sigma_now, D), seq_pos * dim_seq, dim_seq)
    cond_vec = jax.nn.silu(pooled_vector[0] + embedded).astype(jnp.bfloat16)[None]
    mod_terms = jnp.dot(
        cond_vec, mod_weight.reshape(dim_seq, 3 * dim_local), preferred_element_type=jnp.float32
    )
    placed = lax.dynamic_update_slice(
        jnp.zeros((2, 3, D), jnp.float32),
        mod_terms.reshape(1, 3, dim_local),
        (cfg_pos, 0, wblk_pos * dim_local),
    )
    modulation = lax.psum(placed, ("cfg", "seq", "wblk"))

    def standard(rows):
        hidden = rows.astype(jnp.float32)
        average = jnp.mean(hidden, axis=-1, keepdims=True)
        variance = jnp.mean(hidden * hidden, axis=-1, keepdims=True) - average * average
        return average, lax.rsqrt(variance + epsilon)

    image_mean, image_rstd = standard(image_full)
    text_mean, text_rstd = standard(text_full)
    rows_both = jnp.concatenate(
        [jnp.broadcast_to(image_full[None], (2,) + image_full.shape), text_full], axis=2
    )
    mean_both = jnp.concatenate(
        [jnp.broadcast_to(image_mean[None], (2,) + image_mean.shape), text_mean], axis=2
    )
    rstd_both = jnp.concatenate(
        [jnp.broadcast_to(image_rstd[None], (2,) + image_rstd.shape), text_rstd], axis=2
    )
    normed = (
        (rows_both.astype(jnp.float32) - mean_both)
        * rstd_both
        * (1.0 + modulation[:, 1])[:, None, None]
        + modulation[:, 0][:, None, None]
    ).astype(jnp.bfloat16)

    image_index = seq_pos * image_rows + jnp.arange(image_rows, dtype=jnp.int32)
    zeros = jnp.zeros((text_rows,), jnp.float32)
    height_pos = jnp.concatenate([(image_index // GRID).astype(jnp.float32), zeros])
    width_pos = jnp.concatenate([(image_index % GRID).astype(jnp.float32), zeros])
    angles = jnp.repeat(rotary_angles(height_pos, width_pos), 2, axis=1)
    signs = jnp.where(jnp.arange(HD) % 2 == 0, -1.0, 1.0).astype(jnp.float32)
    gains = jnp.stack([query_gain, key_gain])
    qkv = project_qkv(normed, qkv_full, jnp.cos(angles), jnp.sin(angles) * signs, gains, heads)

    count = 2 * prompts * heads
    qkv = qkv.reshape(count, 3, local_len, HD)
    if count % seq_size == 0:
        own = count // seq_size
        mixed = lax.all_to_all(
            qkv.reshape(seq_size, own, 3, local_len, HD), "seq", split_axis=0, concat_axis=0, tiled=True
        )
        unit_index = seq_pos * own + jnp.arange(own, dtype=jnp.int32)
        live = lengths[(unit_index // heads) % prompts]
        attended = attention(live, mixed, mixed, text_rows)
        attended = lax.all_to_all(attended, "seq", split_axis=0, concat_axis=0, tiled=True)
    else:
        keys_values = lax.all_gather(qkv, "seq", axis=0)
        live = lengths[(jnp.arange(count, dtype=jnp.int32) // heads) % prompts]
        attended = attention(live, qkv[None], keys_values, text_rows)
    attended = attended.reshape(2, prompts, heads, local_len, HD)

    mlp_units = jnp.dot(
        normed.reshape(2 * prompts * local_len, D), up_full, preferred_element_type=jnp.float32
    )
    activated = jax.nn.gelu(mlp_units, approximate=True).astype(jnp.bfloat16)
    activated = activated.reshape(2, prompts, local_len, units)

    guided = guided_terms(attended, activated, out_full, modulation[:, 2], image_rows)
    text_att = attended[:, :, :, image_rows:].transpose(0, 1, 3, 2, 4)
    text_att = text_att.reshape(2, prompts, text_rows, heads * HD)
    text_in = jnp.concatenate([text_att, activated[:, :, image_rows:]], axis=-1)
    text_terms = jnp.einsum("cprk,skd->cprsd", text_in, out_full, preferred_element_type=jnp.float32)
    text_terms = text_terms.reshape(2, prompts, text_rows, D).astype(jnp.bfloat16)

    own_prompts = prompts // 2
    image_sum = scatter_features(guided, wblk_pos, wblk_size)
    image_sum = image_sum.reshape((2, own_prompts) + image_sum.shape[1:])
    text_sum = scatter_features(text_terms, wblk_pos, wblk_size)

    def swap_halves(pairs):
        kept = lax.dynamic_index_in_dim(pairs, cfg_pos, 0, keepdims=False)
        given = lax.dynamic_index_in_dim(pairs, 1 - cfg_pos, 0, keepdims=False)
        taken = lax.ppermute(given.astype(jnp.bfloat16), "cfg", [(0, 1), (1, 0)])
        return kept + taken.astype(jnp.float32)

    text_branch = swap_halves(text_sum)
    image_branch = swap_halves(image_sum)
    own_gate = lax.dynamic_slice(modulation, (cfg_pos, 2, wblk_pos * dim_local), (1, 1, dim_local))
    text_out = (text_tokens[0].astype(jnp.float32) + own_gate * text_branch).astype(jnp.bfloat16)[None]
    latent = lax.dynamic_slice_in_dim(image_tokens, cfg_pos * own_prompts, own_prompts, 0).astype(
        jnp.float32
    )
    velocity = latent + image_branch
    new_image = latent + step_size * velocity
    return (text_out, velocity, new_image)


def solution(mesh):
    in_specs = (
        P("cfg", None, "seq", "wblk"),
        P(None, "seq", "wblk"),
        P("cfg", "seq"),
        P("seq", None, "wblk"),
        P("seq", None, "wblk", None),
        P("seq", "wblk"),
        P(),
        P(),
        P("wblk", "seq"),
        P("wblk", "seq"),
        P(),
        P(),
    )
    out_specs = (P("cfg", None, "seq", "wblk"), P("cfg", "seq", "wblk"), P("cfg", "seq", "wblk"))
    sizes = (mesh.shape["cfg"], mesh.shape["seq"], mesh.shape["wblk"])
    return jax.shard_map(
        functools.partial(shards, *sizes),
        mesh=mesh,
        in_specs=in_specs,
        out_specs=out_specs,
        check_vma=False,
    )
```

time: 1210 us -> 938 us (0.78)
  waiting for transfers between devices: 778 us -> 556 us
  matrix products: 235 us -> 38 us
  Pallas kernels: 0 us -> 132 us
  other arithmetic: 84.3 us -> 129 us
  blocking collectives: 36.5 us -> 0 us
  starting transfers between devices: 5.53 us -> 22.1 us
    all_gather x7 -> x3, waiting for transfers between devices: 633 us -> 0.05 us  [the longest x1 0.03 us: shards(): up_full = lax.all_gather(up_part, 'seq', axis=0, tiled=True)]
    dot_general x6 -> x2, matrix products: 232 us -> 34.9 us  [the longest x1 31 us: shards(): jnp.dot(normed.reshape(2 * prompts * local_len, D), up_full, preferred_el...]
    all_to_all x1 -> x2, waiting for transfers between devices: 34.6 us -> 220 us  [the longest x1 197 us: shards(): lax.all_to_all(qkv.reshape(seq_size, own, 3, local_len, HD), 'seq', split...]
    ppermute x0 -> x15, waiting for transfers between devices: none -> 177 us  [the longest x2 67.5 us: gather_features(): far = lax.ppermute(block, 'wblk', CHIP_SWAP)]
    psum x0 -> x1, waiting for transfers between devices: none -> 159 us  [shards(): modulation = lax.psum(placed, ('cfg', 'seq', 'wblk'))]
    pallas_call x0 -> x3, Pallas kernels: none -> 132 us  [the longest x1 66 us: attention(): pl.pallas_call(functools.partial(attention_body, shards_of, rows, text_ro...]
    reduce_scatter x1 -> x0, waiting for transfers between devices: 108 us -> none  [shards(): lax.psum_scatter(branch_terms.reshape(prompts, local_len, D).astype(jnp.b...]
    convert_element_type x2 -> x5, other arithmetic: 5.09 us -> 89 us  [the longest x2 54.7 us: shards(): normed = ((rows_both.astype(jnp.float32) - mean_both) * rstd_both * (1.0...]
  transfers between devices with their start and end apart: 9 -> 21, of which waited for: 8 -> 11; matrix products, arithmetic and copies ran while one was open for 27% -> 20% of each run, Pallas kernels for 0% -> 11%
where the time goes in v1:
time: 938 us; the launch traced here: 937 us
  waiting for transfers between devices  556 us (59%)
  Pallas kernels  132 us (14%)
  other arithmetic  129 us (14%)
  local copies, waits for them, and re-layouts  42.9 us (5%)
  matrix products  38 us (4%)
  starting transfers between devices  22.1 us (2%)
  between operations  17.1 us (2%)
    all_to_all x1, waiting for transfers between devices, shards(): lax.all_to_all(qkv.reshape(seq_size, own, 3, local_len, HD), 'seq', split...  197 us
    psum x1, waiting for transfers between devices, shards(): modulation = lax.psum(placed, ('cfg', 'seq', 'wblk'))  159 us
    ppermute x2, waiting for transfers between devices, gather_features(): far = lax.ppermute(block, 'wblk', CHIP_SWAP)  67.5 us
    ppermute x2, waiting for transfers between devices, scatter_features(): lax.ppermute(far_part.astype(jnp.bfloat16), 'wblk', CHIP_SWAP)  66.4 us
    pallas_call x1, Pallas kernels, attention(): pl.pallas_call(functools.partial(attention_body, shards_of, rows, text_ro...  66 us
    convert_element_type x2, other arithmetic, shards(): normed = ((rows_both.astype(jnp.float32) - mean_both) * rstd_both * (1.0...  54.7 us
    pallas_call x1, Pallas kernels, project_qkv(): pl.pallas_call(functools.partial(qkv_body, heads), grid=grid, in_specs=[p...  34.2 us
    pallas_call x1, Pallas kernels, guided_terms(): pl.pallas_call(functools.partial(guided_body, heads, col_blocks), grid=(p...  32.1 us
  transfers between devices with their start and end apart: 21, of which 11 were waited for; matrix products, arithmetic and copies ran while one was open for 20% of the time, Pallas kernels for 11%

profile of v1, /device:TPU:0, one launch (start us, length us, event | category | flops | bytes accessed | tf_op | source)
XLA Modules:
  0.0 937.1 jit_solution(2981015134575975677)
XLA Ops:
  9.0 0.7 reduce
  9.8 6.1 copy.17
  15.9 3.0 fusion.12
  19.4 0.6 copy-done.9
  20.1 1.2 constant_dynamic-slice_fusion.7
  21.3 2.0 copy.27
  23.3 1.5 copy.19
  25.0 3.0 collective-permute-start
  28.0 1.5 collective-permute-start.3
  29.5 2.4 constant_dynamic-slice_fusion.6
  32.1 7.8 collective-permute-done.3
  40.4 1.0 fusion.21
  42.3 55.3 %collective-permute-done = bf16[2,1024,768]{2,1,0:T(8,128)(2,1)} collective-permute-done((bf16[2,1024,768]{2,1,0:T(8,128)(2,1)}, bf16[2,1024,768]{2,1,0:T(8,128)(2,1)}, u32[]{:S(2)}, u32[]{:S(2)}) %collective-permute-start) | collective-permute-done | bytes 3145760 | tf_op jit(solution)/shard_map/ppermute | solution.py:224
  97.5 0.9 broadcast_multiply_fusion.sin_ref
  99.0 1.0 copy.21.cos_ref
  100.1 0.5 collective-permute-start.6
  100.6 0.6 pad_maximum_fusion.4.gain_ref
  101.2 12.2 %collective-permute-done.4 = bf16[2,2,128,768]{3,2,1,0:T(8,128)(2,1)S(1)} collective-permute-done((bf16[2,2,128,768]{3,2,1,0:T(8,128)(2,1)S(1)}, bf16[2,2,128,768]{3,2,1,0:T(8,128)(2,1)S(1)}, u32[]{:S(2)}, u32[]{:S(2)}) %collective-permute-start.4) | collective-permute-done | bytes 786464 | tf_op jit(solution)/shard_map/ppermute | solution.py:224
  113.4 158.9 %all-reduce.4.cloned.1.call-done = f32[2,3,3072]{2,0,1:T(2,128)} async-done(((f32[2,3,3072]{2,0,1:T(2,128)}), f32[2,3,3072]{2,0,1:T(2,128)}) %all-reduce.4.cloned.1.call-update) | async-done | bytes 73744 | tf_op jit(solution)/shard_map/psum | solution.py:314
  272.3 1.4 slice_bitcast_fusion.1
  273.7 1.7 maximum_select_fusion.5
  275.4 1.9 maximum_select_fusion.4
  277.3 2.6 convert_reduce_fusion.1
  279.9 4.3 maximum_select_fusion.2
  284.3 5.7 maximum_select_fusion.1
  290.0 6.5 convert_reduce_fusion
  296.6 10.8 %broadcast_in_dim.23 = bf16[2,2,1024,3072]{3,2,1,0:T(8,128)(2,1)} broadcast(bf16[2,1024,3072]{2,1,0:T(8,128)(2,1)S(1)} %get-tuple-element.9), dimensions={1,2,3} | broadcast | bytes 37748736 | tf_op jit(solution)/shard_map/broadcast_in_dim | solution.py:325
  307.3 27.0 %add_convert_fusion.x_ref = bf16[2,2,1152,3072]{3,2,1,0:T(8,128)(2,1)} fusion(f32[2,3072]{1,0:T(2,128)S(1)} %get-tuple-element.18, f32[2,3072]{1,0:T(2,128)S(1)} %get-tuple-element.19, f32[2,2,1152]{2,1,0:T(2,128)S(1)} %get-tuple-element.22, f32[2,2,1152]{2,1,0:T(2,128)S(1)} %get-tuple-element.33, bf16[2,2,128,3072]{3,2,1,0:T(8,128)(2,1)} %get-tuple-element.10, ...), kind=kLoop, calls=%fused_computation.6 | loop fusion | flops 127401984 | bytes 56709120 | tf_op jit(solution)/shard_map/convert_element_type | solution.py:338
  334.4 34.2 %project_qkv.1 = bf16[2,2,2,3,1152,128]{5,4,3,2,1,0:T(8,128)(2,1)} custom-call(bf16[2,2,1152,3072]{3,2,1,0:T(8,128)(2,1)} %add_convert_fusion.x_ref, bf16[3072,768]{1,0:T(8,128)(2,1)} %all-gather.5.cloned.1.call-done.w_ref, f32[1152,128]{1,0:T(8,128)} %copy.21.cos_ref, f32[1152,128]{1,0:T(8,128)} %broadcast_multiply_fusion.sin_ref, ...), custom_call_target="tpu_custom_call" | custom-call | flops 21743271936 | bytes 33030144 | tf_op jit(solution)/shard_map/project_qkv/pallas_call | solution.py:85
  368.6 6.6 all-to-all-start
  375.2 1.4 constant_dynamic-slice_fusion.4
  376.6 1.2 pad_maximum_fusion
  377.9 1.2 gather_fusion
  379.1 27.8 %maximum_convert_fusion = f32[2,2,1152,3072]{3,2,1,0:T(8,128)} fusion(bf16[2,2,128,3072]{3,2,1,0:T(8,128)(2,1)} %get-tuple-element.10, bf16[2,2,1024,3072]{3,2,1,0:T(8,128)(2,1)} %broadcast_in_dim.23), kind=kLoop, calls=%fused_computation.9 | loop fusion | flops 56623104 | bytes 84934656 | tf_op jit(solution)/shard_map/convert_element_type | solution.py:334
  406.9 27.6 %fusion = bf16[4608,3072]{1,0:T(8,128)(2,1)} fusion(f32[2,2,1152,3072]{3,2,1,0:T(8,128)} %maximum_convert_fusion, f32[4608]{0:T(1024)S(1)} %mul.240, f32[4608]{0:T(1024)S(1)} %sub.76, f32[2,3072]{1,0:T(2,128)S(1)} %get-tuple-element.18, f32[2,3072]{1,0:T(2,128)S(1)} %get-tuple-element.19), kind=kLoop, calls=%fused_computation.2 | loop fusion | flops 70778880 | bytes 85020672 | tf_op jit(solution)/shard_map/convert_element_type | solution.py:338
  434.6 197.2 %all-to-all-done.q_ref.k_ref.v_ref = bf16[4,2,3,1152,128]{4,3,2,1,0:T(8,128)(2,1)} async-done(((bf16[4,2,3,1152,128]{4,3,2,1,0:T(8,128)(2,1)}), bf16[4,2,3,1152,128]{4,3,2,1,0:T(8,128)(2,1)}, u32[]{:S(2)}, u32[]{:S(2)}) %all-to-all-start) | async-done | bytes 7077920 | tf_op jit(solution)/shard_map/all_to_all | solution.py:353
  631.8 66.0 %attention.1 = bf16[4,2,1152,128]{3,2,1,0:T(8,128)(2,1)} custom-call(s32[2]{0:T(128)} %gather_fusion, bf16[4,2,3,1152,128]{4,3,2,1,0:T(8,128)(2,1)} %all-to-all-done.q_ref.k_ref.v_ref, bf16[4,2,3,1152,128]{4,3,2,1,0:T(8,128)(2,1)} %all-to-all-done.q_ref.k_ref.v_ref, bf16[4,2,3,1152,128]{4,3,2,1,0:T(8,128)(2,1)} %all-to-all-done.q_ref.k_ref.v_ref), custom_call_target="tpu_custom_call" | custom-call | flops 21743271936 | bytes 9437184 | tf_op jit(solution)/shard_map/attention/pallas_call | solution.py:152
  697.8 3.6 all-to-all-start.1
  701.5 31.0 %fusion.10 = bf16[4608,768]{1,0:T(8,128)(2,1)} fusion(bf16[4608,3072]{1,0:T(8,128)(2,1)} %fusion, bf16[3072,768]{1,0:T(8,128)(2,1)} %all-gather.7.cloned.1.call-done), kind=kOutput, calls=%fused_computation.19 | convolution fusion | flops 21775122432 | bytes 40108032 | tf_op jit(solution)/shard_map/dot_general | solution.py:366
  732.5 22.4 %all-to-all-done.1 = bf16[4,2,1152,128]{3,2,1,0:T(8,128)(2,1)S(1)} async-done(((bf16[4,2,1152,128]{3,2,1,0:T(8,128)(2,1)}), bf16[4,2,1152,128]{3,2,1,0:T(8,128)(2,1)S(1)}, u32[]{:S(2)}, u32[]{:S(2)}) %all-to-all-start.1) | async-done | bytes 2359328 | tf_op jit(solution)/shard_map/all_to_all | solution.py:359
  754.9 1.4 copy-done.6
  756.3 32.1 %guided_terms.1 = bf16[2,1024,3072]{2,1,0:T(8,128)(2,1)} custom-call(bf16[2,2,2,1152,128]{4,3,2,1,0:T(8,128)(2,1)} %bitcast.107, bf16[2,2,1152,768]{3,2,1,0:T(8,128)(2,1)} %bitcast.111, bf16[4,1024,768]{2,1,0:T(8,128)(2,1)} %bitcast.116, f32[2,3072]{1,0:T(2,128)} %get-tuple-element.17.gate_ref), custom_call_target="tpu_custom_call" | custom-call | flops 25769803776 | bytes 27262976 | tf_op jit(solution)/shard_map/guided_terms/pallas_call | solution.py:196
  788.4 6.0 constant_dynamic-slice_fusion.1
  794.3 0.5 collective-permute-start.11
  794.8 5.5 collective-permute-done.12
  800.3 5.3 add_convert_fusion.1
  805.6 1.6 collective-permute-start.13
  807.2 1.2 slice.25
  808.4 1.0 copy_bitcast_fusion
  809.4 3.9 convert_bitcast_fusion
  813.7 1.7 copy-done.3
  816.1 1.8 collective-permute-done.8
  817.9 1.3 add_convert_fusion.2
  819.2 0.5 collective-permute-start.9
  819.7 57.1 %collective-permute-done.13 = bf16[2,1024,768]{2,1,0:T(8,128)(2,1)} collective-permute-done((bf16[2,1024,768]{2,1,0:T(8,128)(2,1)}, bf16[2,1024,768]{2,1,0:T(8,128)(2,1)}, u32[]{:S(2)}, u32[]{:S(2)}) %collective-permute-start.13) | collective-permute-done | bytes 3145760 | tf_op jit(solution)/shard_map/ppermute | solution.py:250
  876.8 5.0 convert_add_fusion
  882.0 1.5 collective-permute-start.14
  883.5 9.2 collective-permute-done.9
  892.8 1.4 convert_add_fusion.3
  894.2 1.5 collective-permute-start.10
  895.8 0.8 dynamic-slice_reduce_fusion
  896.6 28.5 %collective-permute-done.10 = bf16[2,128,768]{2,1,0:T(8,128)(2,1)S(1)} collective-permute-done((bf16[2,128,768]{2,1,0:T(8,128)(2,1)S(1)}, bf16[2,128,768]{2,1,0:T(8,128)(2,1)S(1)}, u32[]{:S(2)}, u32[]{:S(2)}) %collective-permute-start.10) | collective-permute-done | bytes 393248 | tf_op jit(solution)/shard_map/ppermute | solution.py:387
  925.1 0.9 fusion.20
  926.0 3.5 convert_add_fusion.1
  (89 shorter events, 4.7 us)
Async XLA Ops:
  8.0 12.1 %copy-start = (bf16[768,3,4,128]{3,2,1,0:T(4,128)(2,1)S(1)}, bf16[768,3,4,128]{3,2,1,0:T(4,128)(2,1)}, u32[]{:S(2)}) copy-start(bf16[768,3,4,128]{3,2,1,0:T(4,128)(2,1)} %param.16) | copy-start | bytes 7077892
  8.0 264.3 %all-reduce.4.cloned.1.call-start = ((), (), s32[]{:S(2)}) async-start(), calls=%async_computation.2 | async-start | bytes 147456 | tf_op jit(solution)/shard_map/psum | solution.py:314
  19.3 0.6 copy-start.9
  20.0 314.4 %all-gather.5.cloned.1.call-start = ((), (), s32[]{:S(2)}) async-start(), calls=%async_computation.3 | async-start | bytes 5898240 | tf_op jit(solution)/shard_map/all_gather | solution.py:284
  21.3 18.6 %copy-start.7 = (bf16[1,2,128,768]{3,2,1,0:T(8,128)(2,1)S(1)}, bf16[1,2,128,768]{3,2,1,0:T(8,128)(2,1)}, u32[]{:S(2)}) copy-start(bf16[1,2,128,768]{3,2,1,0:T(8,128)(2,1)} %param.12) | copy-start | bytes 1179652
  24.8 676.7 %all-gather.7.cloned.1.call-start = ((), (), s32[]{:S(2)}) async-start(), calls=%async_computation.4 | async-start | bytes 5898240 | tf_op jit(solution)/shard_map/all_gather | solution.py:286
  25.0 72.5 %collective-permute-start = (bf16[2,1024,768]{2,1,0:T(8,128)(2,1)}, bf16[2,1024,768]{2,1,0:T(8,128)(2,1)}, u32[]{:S(2)}, u32[]{:S(2)}) collective-permute-start(bf16[2,1024,768]{2,1,0:T(8,128)(2,1)} %param.13), channel_id=1, source_target_pairs={{0,2},{2,0},{1,3},{3,1},{4,6},{6,4},{5,7},{7,5},{8,10},{10,8},{9,1... | collective-permute-start | bytes 9437192 | tf_op jit(solution)/shard_map/ppermute | solution.py:224
  28.0 251.9 %collective-permute-start.2 = (bf16[2,1024,768]{2,1,0:T(8,128)(2,1)}, bf16[2,1024,768]{2,1,0:T(8,128)(2,1)}, u32[]{:S(2)}, u32[]{:S(2)}) collective-permute-start(bf16[2,1024,768]{2,1,0:T(8,128)(2,1)} %param.13), channel_id=1, source_target_pairs={{0,1},{1,0},{2,3},{3,2},{4,5},{5,4},{6,7},{7,6},{8,9},{9,8},{10,11... | collective-permute-start | bytes 9437192 | tf_op jit(solution)/shard_map/ppermute | solution.py:225
  28.0 11.8 %collective-permute-start.3 = (bf16[2,128,768]{2,1,0:T(8,128)(2,1)}, bf16[2,128,768]{2,1,0:T(8,128)(2,1)S(1)}, u32[]{:S(2)}, u32[]{:S(2)}) collective-permute-start(bf16[2,128,768]{2,1,0:T(8,128)(2,1)} %bitcast.109), channel_id=1, source_target_pairs={{0,16},{16,0},{1,17},{17,1},{2,18},{18,2},{3,19},{19,3},{4,20},{20... | collective-permute-start | bytes 1179656 | tf_op jit(solution)/shard_map/ppermute | solution.py:296
  39.9 60.7 %copy-start.11 = (f32[128]{0:T(128)S(1)}, f32[128]{0:T(128)}, u32[]{:S(2)}) copy-start(f32[128]{0:T(128)} %param.19) | copy-start | bytes 1540
  39.9 60.7 %copy-start.12 = (f32[128]{0:T(128)S(1)}, f32[128]{0:T(128)}, u32[]{:S(2)}) copy-start(f32[128]{0:T(128)} %param.18) | copy-start | bytes 1540
  40.0 73.4 %collective-permute-start.4 = (bf16[2,2,128,768]{3,2,1,0:T(8,128)(2,1)S(1)}, bf16[2,2,128,768]{3,2,1,0:T(8,128)(2,1)S(1)}, u32[]{:S(2)}, u32[]{:S(2)}) collective-permute-start(bf16[2,2,128,768]{3,2,1,0:T(8,128)(2,1)S(1)} %maximum_select_fusion.6), channel_id=1, source_target_pairs={{0,2},{2,0},{1,3},{3,1},{4,6},{6,4},{5,7},{7,5},{8,10},{10,8},{9,1... | collective-permute-start | bytes 2359304 | tf_op jit(solution)/shard_map/ppermute | solution.py:224
  97.5 186.7 %collective-permute-start.1 = (bf16[2,1024,768]{2,1,0:T(8,128)(2,1)}, bf16[2,1024,768]{2,1,0:T(8,128)(2,1)}, u32[]{:S(2)}, u32[]{:S(2)}) collective-permute-start(bf16[2,1024,768]{2,1,0:T(8,128)(2,1)} %collective-permute-done), channel_id=1, source_target_pairs={{0,1},{1,0},{2,3},{3,2},{4,5},{5,4},{6,7},{7,6},{8,9},{9,8},{10,11... | collective-permute-start | bytes 9437192 | tf_op jit(solution)/shard_map/ppermute | solution.py:226
  100.1 173.6 %collective-permute-start.6 = (bf16[2,2,128,768]{3,2,1,0:T(8,128)(2,1)S(1)}, bf16[2,2,128,768]{3,2,1,0:T(8,128)(2,1)}, u32[]{:S(2)}, u32[]{:S(2)}) collective-permute-start(bf16[2,2,128,768]{3,2,1,0:T(8,128)(2,1)S(1)} %maximum_select_fusion.6), channel_id=1, source_target_pairs={{0,1},{1,0},{2,3},{3,2},{4,5},{5,4},{6,7},{7,6},{8,9},{9,8},{10,11... | collective-permute-start | bytes 2359304 | tf_op jit(solution)/shard_map/ppermute | solution.py:225
  113.4 162.0 %collective-permute-start.5 = (bf16[2,2,128,768]{3,2,1,0:T(8,128)(2,1)S(1)}, bf16[2,2,128,768]{3,2,1,0:T(8,128)(2,1)}, u32[]{:S(2)}, u32[]{:S(2)}) collective-permute-start(bf16[2,2,128,768]{3,2,1,0:T(8,128)(2,1)S(1)} %collective-permute-done.4), channel_id=1, source_target_pairs={{0,1},{1,0},{2,3},{3,2},{4,5},{5,4},{6,7},{7,6},{8,9},{9,8},{10,11... | collective-permute-start | bytes 2359304 | tf_op jit(solution)/shard_map/ppermute | solution.py:226
  275.4 4.5 copy-start.4
  368.6 6.6 copy-start.10
  368.6 263.2 %all-to-all-start = ((bf16[4,2,3,1152,128]{4,3,2,1,0:T(8,128)(2,1)}), bf16[4,2,3,1152,128]{4,3,2,1,0:T(8,128)(2,1)}, u32[]{:S(2)}, u32[]{:S(2)}) async-start(bf16[4,2,3,1152,128]{4,3,2,1,0:T(8,128)(2,1)} %bitcast.105), calls=%async_computation | async-start | bytes 14155776 | tf_op jit(solution)/shard_map/all_to_all | solution.py:353
  375.2 2.8 copy-start.2
  375.2 357.3 %all-gather.9.cloned.1.call-start = ((), (), s32[]{:S(2)}) async-start(), calls=%async_computation.5 | async-start | bytes 7864320 | tf_op jit(solution)/shard_map/all_gather | solution.py:294
  697.8 57.1 %all-to-all-start.1 = ((bf16[4,2,1152,128]{3,2,1,0:T(8,128)(2,1)}), bf16[4,2,1152,128]{3,2,1,0:T(8,128)(2,1)S(1)}, u32[]{:S(2)}, u32[]{:S(2)}) async-start(bf16[4,2,1152,128]{3,2,1,0:T(8,128)(2,1)} %attention.1), calls=%async_computation.1 | async-start | bytes 4718592 | tf_op jit(solution)/shard_map/all_to_all | solution.py:359
  754.9 1.4 copy-start.6
  794.3 6.0 collective-permute-start.12
  794.3 15.0 %slice-start = ((s8[6291456]{0:T(1024)(128)(4,1)}), s8[4194304]{0:T(1024)(128)(4,1)S(1)}, s32[]{:S(2)}) async-start(s8[6291456]{0:T(1024)(128)(4,1)} %bitcast.117), calls=%async_computation.6 | async-start | bytes 8388608
  794.3 15.0 %slice-start.1 = ((s8[6291456]{0:T(1024)(128)(4,1)}), s8[2097152]{0:T(1024)(128)(4,1)S(1)}, s32[]{:S(2)}) async-start(s8[6291456]{0:T(1024)(128)(4,1)} %bitcast.117), calls=%async_computation.7 | async-start | bytes 4194304
  794.3 25.4 %collective-permute-start.11 = (bf16[2,1024,768]{2,1,0:T(8,128)(2,1)}, bf16[2,1024,768]{2,1,0:T(8,128)(2,1)}, u32[]{:S(2)}, u32[]{:S(2)}) collective-permute-start(bf16[2,1024,768]{2,1,0:T(8,128)(2,1)} %get-tuple-element.11), channel_id=1, source_target_pairs={{0,1},{1,0},{2,3},{3,2},{4,5},{5,4},{6,7},{7,6},{8,9},{9,8},{10,11... | collective-permute-start | bytes 9437192 | tf_op jit(solution)/shard_map/ppermute | solution.py:251
  805.6 71.3 %collective-permute-start.13 = (bf16[2,1024,768]{2,1,0:T(8,128)(2,1)}, bf16[2,1024,768]{2,1,0:T(8,128)(2,1)}, u32[]{:S(2)}, u32[]{:S(2)}) collective-permute-start(bf16[2,1024,768]{2,1,0:T(8,128)(2,1)} %add_convert_fusion.1), channel_id=1, source_target_pairs={{0,2},{2,0},{1,3},{3,1},{4,6},{6,4},{5,7},{7,5},{8,10},{10,8},{9,1... | collective-permute-start | bytes 9437192 | tf_op jit(solution)/shard_map/ppermute | solution.py:250
  813.7 1.7 copy-start.3
  815.5 2.4 collective-permute-start.8
  815.6 67.9 %collective-permute-start.7 = (bf16[2,2,128,768]{3,2,1,0:T(8,128)(2,1)S(1)}, bf16[2,2,128,768]{3,2,1,0:T(8,128)(2,1)S(1)}, u32[]{:S(2)}, u32[]{:S(2)}) collective-permute-start(bf16[2,2,128,768]{3,2,1,0:T(8,128)(2,1)S(1)} %get-tuple-element.13), channel_id=1, source_target_pairs={{0,1},{1,0},{2,3},{3,2},{4,5},{5,4},{6,7},{7,6},{8,9},{9,8},{10,11... | collective-permute-start | bytes 2359304 | tf_op jit(solution)/shard_map/ppermute | solution.py:251
  819.2 73.6 %collective-permute-start.9 = (bf16[2,2,128,768]{3,2,1,0:T(8,128)(2,1)S(1)}, bf16[2,2,128,768]{3,2,1,0:T(8,128)(2,1)S(1)}, u32[]{:S(2)}, u32[]{:S(2)}) collective-permute-start(bf16[2,2,128,768]{3,2,1,0:T(8,128)(2,1)S(1)} %add_convert_fusion.2), channel_id=1, source_target_pairs={{0,2},{2,0},{1,3},{3,1},{4,6},{6,4},{5,7},{7,5},{8,10},{10,8},{9,1... | collective-permute-start | bytes 2359304 | tf_op jit(solution)/shard_map/ppermute | solution.py:250
  881.8 43.3 %copy-start.8 = (bf16[1,2,128,768]{3,2,1,0:T(8,128)(2,1)S(1)}, bf16[1,2,128,768]{3,2,1,0:T(8,128)(2,1)}, u32[]{:S(2)}) copy-start(bf16[1,2,128,768]{3,2,1,0:T(8,128)(2,1)} %param.12) | copy-start | bytes 1179652
  881.8 44.2 %copy-start.5 = (bf16[2,1024,768]{2,1,0:T(8,128)(2,1)S(1)}, bf16[2,1024,768]{2,1,0:T(8,128)(2,1)}, u32[]{:S(2)}) copy-start(bf16[2,1024,768]{2,1,0:T(8,128)(2,1)} %param.13) | copy-start | bytes 9437188
  882.0 44.0 %collective-permute-start.14 = (bf16[1,1024,768]{2,1,0:T(8,128)(2,1)S(1)}, bf16[1,1024,768]{2,1,0:T(8,128)(2,1)S(1)}, u32[]{:S(2)}, u32[]{:S(2)}) collective-permute-start(bf16[1,1024,768]{2,1,0:T(8,128)(2,1)S(1)} %dynamic-slice_convert_fusion), channel_id=1, source_target_pairs={{0,16},{16,0},{1,17},{17,1},{2,18},{18,2},{3,19},{19,3},{4,20},{20... | collective-permute-start | bytes 4718600 | tf_op jit(solution)/shard_map/ppermute | solution.py:387
  894.2 30.9 %collective-permute-start.10 = (bf16[2,128,768]{2,1,0:T(8,128)(2,1)S(1)}, bf16[2,128,768]{2,1,0:T(8,128)(2,1)S(1)}, u32[]{:S(2)}, u32[]{:S(2)}) collective-permute-start(bf16[2,128,768]{2,1,0:T(8,128)(2,1)S(1)} %fusion.19), channel_id=1, source_target_pairs={{0,16},{16,0},{1,17},{17,1},{2,18},{18,2},{3,19},{19,3},{4,20},{20... | collective-permute-start | bytes 1179656 | tf_op jit(solution)/shard_map/ppermute | solution.py:387
  926.0 3.5 copy-start.1
Sparse Core Ops, SparseCore 0:
  20.1 252.1 all-reduce.3
Sparse Core Ops, SparseCore 1:
  24.9 92.2 all-gather.4
  118.6 88.1 all-gather.6
  377.9 229.7 all-gather.8
